TPU v7x, 32 devices: a whole 2x2x4 slice. The times are simulated.
32 devices in a mesh: tm: 8 (over y, x, core), freq: 4 (over z).
Axes of the slice: x: 2, y: 2, z: 4, core: 2. Of those that a mesh axis runs over, the one named last changes fastest.
Arguments:
- records: bfloat16 [524288, 1024], P('tm', 'freq'), may hold values from -6 to 6
- bins: int32 [32], P('freq'), may hold values from 0 to 4095, as said below
- loads: bfloat16 [2, 64, 1024], P(None, None, 'tm'), may hold values from -0.1875 to 0.1875
Outputs:
- csd: float32 [1024, 32, 2, 1024], P('tm', 'freq')
- psd: float32 [2, 32, 64, 64], P(None, 'freq', 'tm')
Inputs may be any that keep to these rules, and one draw needn't show every extreme that they name: The 32 entries are distinct; entries 8 f to 8 (f + 1) - 1 are the bins owned by index f of freq.
All inputs are finite; a program needn't handle non-finite values.
Results may differ from a plain program's by a relative error of at most 0.0048.
Values may be sent and summed in bfloat16 or wider, within the bound.
A program may use at most 320 MiB of HBM per device.

v0:
```python
import math

import jax
import jax.numpy as jnp
from jax import lax
from jax.sharding import PartitionSpec as P

SEGLEN = 8192


def shifted(value, axis, steps):
    count = lax.axis_size(axis)
    first, last = (max(0, -steps), min(count, count - steps))
    return lax.ppermute(value, axis, [(source, source + steps) for source in range(first, last)])


def make_table(bin_ids):
    positions = lax.iota(jnp.int32, SEGLEN)
    turns = bin_ids[:, None] * positions[None, :] % SEGLEN
    angle = 2.0 * math.pi / SEGLEN * turns.astype(jnp.float32)
    window = 0.5 - 0.5 * jnp.cos(2.0 * math.pi / SEGLEN * positions.astype(jnp.float32))
    table = jnp.concatenate(
        [window[None, :] * jnp.cos(angle), -window[None, :] * jnp.sin(angle)], axis=0
    )
    return (table.astype(jnp.bfloat16), jnp.sum(window * window))


def cross_rows(left, right):
    turned = jnp.stack([left[:, 1], -left[:, 0]], axis=1)
    real = jnp.einsum("spbi,spbj->ibj", left, right, preferred_element_type=jnp.float32)
    imag = jnp.einsum("spbi,spbj->ibj", turned, right, preferred_element_type=jnp.float32)
    return jnp.stack([real, imag], axis=2)


def per_device(records, bins, loads):
    highest = lax.Precision.HIGHEST
    tm_count = lax.axis_size("tm")
    all_bins = lax.all_gather(bins, "freq", axis=0, tiled=True)
    table, energy = make_table(all_bins)
    half = SEGLEN // 2
    chans = records.shape[1]
    segs = records.shape[0] // half
    nbins = all_bins.shape[0]
    halves = records.reshape(segs, half, chans)
    following = shifted(records[:half], "tm", -1)
    seconds = jnp.concatenate([halves[1:], following[None]], axis=0)
    frames = jnp.concatenate([halves, seconds], axis=1)
    spec = jnp.einsum("kn,snc->skc", table, frames, preferred_element_type=jnp.float32)
    spectra = spec.reshape(segs, 2, nbins, chans).astype(jnp.bfloat16)
    owned = lax.all_to_all(spectra, "freq", split_axis=2, concat_axis=3, tiled=True)
    scale = 1.0 / (segs * tm_count * energy)
    csd = lax.psum_scatter(cross_rows(owned, owned) * scale, "tm", scatter_dimension=0, tiled=True)
    whole = lax.all_gather(loads, "tm", axis=2, tiled=True).astype(jnp.float32)
    mine = loads.astype(jnp.float32)
    q_real = jnp.einsum("ibj,mj->ibm", csd[:, :, 0], whole[0], precision=highest) + jnp.einsum(
        "ibj,mj->ibm", csd[:, :, 1], whole[1], precision=highest
    )
    q_imag = jnp.einsum("ibj,mj->ibm", csd[:, :, 1], whole[0], precision=highest) - jnp.einsum(
        "ibj,mj->ibm", csd[:, :, 0], whole[1], precision=highest
    )
    p_real = jnp.einsum("li,ibm->blm", mine[0], q_real, precision=highest) - jnp.einsum(
        "li,ibm->blm", mine[1], q_imag, precision=highest
    )
    p_imag = jnp.einsum("li,ibm->blm", mine[0], q_imag, precision=highest) + jnp.einsum(
        "li,ibm->blm", mine[1], q_real, precision=highest
    )
    terms = jnp.stack([p_real, p_imag], axis=0)
    psd = lax.psum_scatter(terms, "tm", scatter_dimension=2, tiled=True)
    return (csd, psd)


def solution(mesh):
    placed = (P("tm", "freq"), P("freq"), P(None, None, "tm"))
    return jax.shard_map(
        per_device,
        mesh=mesh,
        in_specs=placed,
        out_specs=(P("tm", "freq", None, None), P(None, "freq", "tm", None)),
        check_vma=False,
    )
```

profile of v0, /device:TPU:0, one launch (start us, length us, event | category | flops | bytes accessed | tf_op | source)
XLA Modules:
  0.0 628.2 jit_solution(9634825849414174348)
XLA Ops:
  7.2 1.7 slice.41
  8.9 1.3 collective-permute-start
  10.2 21.4 %slice.39 = bf16[61440,256]{1,0:T(8,128)(2,1)} slice(bf16[65536,256]{1,0:T(8,128)(2,1)} %param.3), slice={[4096:65536], [0:256]} | slice | bytes 62914560 | tf_op jit(solution)/shard_map/slice | solution.py:46
  33.1 9.9 %all-reduce = s32[32]{0:T(128)S(1)} all-reduce(s32[32]{0:T(128)S(1)} %dynamic-update-slice), channel_id=1, replica_groups=mesh['tm'=8,'freq'=4] {'freq'}, use_global_device_ids=true, to_apply=%add | all-reduce | flops 32 | bytes 256
  43.1 4.3 multiply_convert_fusion.1
  47.5 45.7 %fusion.10 = bf16[16,256,64]{1,2,0:T(8,128)(2,1)S(1)} fusion(bf16[1,4096,256]{2,1,0:T(8,128)(2,1)} %bitcast.2, bf16[15,4096,256]{2,1,0:T(8,128)(2,1)} %bitcast.82, bf16[16,4096,256]{2,1,0:T(8,128)(2,1)} %bitcast.81, bf16[32,8192]{1,0:T(8,128)(2,1)S(1)} %get-tuple-element.9, bf16[32,8192]{1,0:T(8,128)(2,1)S(1)} %get-tuple-element.8), kind=kOutput, calls=%fused_computation.18 | convolution fusion | flops 4498653184 | bytes 68681728 | tf_op jit(solution)/shard_map/kn,snc->skc/dot_general | solution.py:48
  93.1 1.3 copy.12
  94.5 3.5 all-to-all-start
  98.2 0.7 multiply_reduce_fusion
  99.6 12.5 %all-to-all-done = bf16[16,2,32,256]{3,1,0,2:T(2,128)(2,1)S(1)} async-done(((bf16[16,2,32,256]{3,1,0,2:T(2,128)(2,1)}), bf16[16,2,32,256]{3,1,0,2:T(2,128)(2,1)S(1)}, u32[]{:S(2)}, u32[]{:S(2)}) %all-to-all-start) | async-done | bytes 524320 | tf_op jit(solution)/shard_map/all_to_all | solution.py:50
  112.9 13.1 %convolution_bitcast_fusion.1 = f32[1024,8,1,1024]{0,3,1,2:T(8,128)} fusion(bf16[16,2,8,1024]{3,0,1,2:T(8,128)(2,1)S(1)} %all_to_all.16), kind=kOutput, calls=%fused_computation.8 | convolution fusion | flops 536870912 | bytes 34078720 | tf_op jit(solution)/shard_map/spbi,spbj->ibj/dot_general | solution.py:30
  126.1 13.2 %convolution_bitcast_fusion = f32[1024,8,1,1024]{0,3,1,2:T(8,128)} fusion(bf16[16,2,8,1024]{3,0,1,2:T(8,128)(2,1)S(1)} %all_to_all.16, bf16[16,1,8,1024]{3,0,1,2:T(8,128)(2,1)S(1)} %get-tuple-element.7, bf16[16,1,8,1024]{3,0,1,2:T(8,128)(2,1)S(1)} %get-tuple-element.6), kind=kOutput, calls=%fused_computation.7 | convolution fusion | flops 537133056 | bytes 34603008 | tf_op jit(solution)/shard_map/spbi,spbj->ibj/dot_general | solution.py:31
  139.2 44.5 %maximum_multiply_fusion = f32[1024,8,2,1024]{0,3,1,2:T(8,128)} fusion(f32[1024,8,1,1024]{0,3,1,2:T(8,128)} %convolution_bitcast_fusion, f32[1024,8,1,1024]{0,3,1,2:T(8,128)} %convolution_bitcast_fusion.1, f32[]{:T(128)S(6)} %div.3), kind=kLoop, calls=%fused_computation.6 | loop fusion | flops 33554432 | bytes 134217728 | tf_op jit(solution)/shard_map/mul | solution.py:52
  183.8 0.7 copy-done
  184.5 10.3 %all_gather.7 = bf16[2,64,1024]{2,1,0:T(8,128)(2,1)S(1)} all-gather(bf16[2,64,128]{2,1,0:T(8,128)(2,1)S(1)} %copy-done), channel_id=1, replica_groups=mesh['tm'=8,'freq'=4] {'tm'}, dimensions={2}, use_global_device_ids=true | all-gather | bytes 294912 | tf_op jit(solution)/shard_map/all_gather | solution.py:53
  194.8 373.2 %reduce-scatter.3.cloned.1.call-done = f32[128,8,2,1024]{0,3,1,2:T(8,128)} async-done(((f32[1024,8,2,1024]{0,3,1,2:T(8,128)}), f32[128,8,2,1024]{0,3,1,2:T(8,128)}) %reduce-scatter.3.cloned.1.call-update) | async-done | bytes 8388624 | tf_op jit(solution)/shard_map/reduce_scatter | solution.py:52
  568.0 3.8 fusion.7
  571.9 3.9 fusion.13
  576.0 3.9 fusion.6
  579.8 3.9 fusion.14
  584.5 1.0 copy.18
  585.6 13.2 %copy.19 = f32[128,8,2,1024]{3,2,1,0:T(2,128)} copy(f32[128,8,2,1024]{0,3,1,2:T(8,128)} %reduce-scatter.3.cloned.1.call-done) | data formatting | bytes 16777216
  598.8 21.1 %reduce-scatter.5.cloned.1.call-done = f32[2,8,8,64]{3,1,0,2:T(8,128)} async-done(((f32[2,8,64,64]{3,1,0,2:T(8,128)}), f32[2,8,8,64]{3,1,0,2:T(8,128)}) %reduce-scatter.5.cloned.1.call-update) | async-done | bytes 32784 | tf_op jit(solution)/shard_map/reduce_scatter | solution.py:68
  619.9 1.5 copy.20
  (22 shorter events, 3.2 us)
Async XLA Ops:
  8.9 38.6 %collective-permute-start = (bf16[4096,256]{1,0:T(8,128)(2,1)S(1)}, bf16[4096,256]{1,0:T(8,128)(2,1)}, u32[]{:S(2)}, u32[]{:S(2)}) collective-permute-start(bf16[4096,256]{1,0:T(8,128)(2,1)S(1)} %slice.41), channel_id=1, source_target_pairs={{4,0},{8,4},{12,8},{16,12},{20,16},{24,20},{28,24},{5,1},{9,5},{13... | collective-permute-start | bytes 6291464 | tf_op jit(solution)/shard_map/ppermute | solution.py:14
  10.2 21.4 %copy-start.2 = (u32[32]{0:T(128)S(1)}, u32[32]{0:T(128)}, u32[]{:S(2)}) copy-start(u32[32]{0:T(128)} %constant.28) | copy-start | bytes 388
  10.2 22.6 %copy-start.1 = (s32[8]{0:T(128)S(1)}, s32[8]{0:T(128)}, u32[]{:S(2)}) copy-start(s32[8]{0:T(128)} %param.4) | copy-start | bytes 100
  94.5 17.6 %all-to-all-start = ((bf16[16,2,32,256]{3,1,0,2:T(2,128)(2,1)}), bf16[16,2,32,256]{3,1,0,2:T(2,128)(2,1)S(1)}, u32[]{:S(2)}, u32[]{:S(2)}) async-start(bf16[16,2,32,256]{3,1,0,2:T(2,128)(2,1)} %copy.12), calls=%async_computation | async-start | bytes 1048576 | tf_op jit(solution)/shard_map/all_to_all | solution.py:50
  98.0 470.1 %reduce-scatter.3.cloned.1.call-start = ((), (), s32[]{:S(2)}) async-start(), calls=%async_computation.3 | async-start | bytes 75497472 | tf_op jit(solution)/shard_map/reduce_scatter | solution.py:52
  183.7 0.8 copy-start
  183.7 436.1 %reduce-scatter.5.cloned.1.call-start = ((), (), s32[]{:S(2)}) async-start(), calls=%async_computation.4 | async-start | bytes 589824 | tf_op jit(solution)/shard_map/reduce_scatter | solution.py:68
Sparse Core Ops, SparseCore 0:
  183.9 384.0 reduce-scatter.2
  585.7 34.1 reduce-scatter.4
where the time goes:
time: 629 us; the launch traced here: 628 us
  waiting for transfers between devices  407 us (65%)
  matrix products  88.4 us (14%)
  other arithmetic  49.8 us (8%)
  local copies, waits for them, and re-layouts  42.5 us (7%)
  blocking collectives  20.2 us (3%)
  between operations  15.5 us (2%)
    reduce_scatter x1, waiting for transfers between devices, per_device(): lax.psum_scatter(cross_rows(owned, owned) * scale, 'tm', scatter_dimensio...  373 us
    dot_general x1, matrix products, per_device(): jnp.einsum('kn,snc->skc', table, frames, preferred_element_type=jnp.float32)  45.7 us
    mul x1, other arithmetic, per_device(): cross_rows(owned, owned) * scale  44.5 us
    slice x1, local copies, waits for them, and re-layouts, per_device(): seconds = jnp.concatenate([halves[1:], following[None]], axis=0)  21.4 us
    reduce_scatter x1, waiting for transfers between devices, per_device(): psd = lax.psum_scatter(terms, 'tm', scatter_dimension=2, tiled=True)  21.1 us
    unnamed x11, local copies, waits for them, and re-layouts  16.2 us
    dot_general x1, matrix products, cross_rows(): jnp.einsum('spbi,spbj->ibj', turned, right, preferred_element_type=jnp.fl...  13.2 us
    dot_general x1, matrix products, cross_rows(): jnp.einsum('spbi,spbj->ibj', left, right, preferred_element_type=jnp.floa...  13.1 us
  transfers between devices with their start and end apart: 4, of which 3 were waited for; matrix products, arithmetic and copies ran while one was open for 6% of the time, Pallas kernels for 0%

commit v1 on v0

v1 whole, which is shorter than its diff:
```python
import math

import jax
import jax.numpy as jnp
from jax import lax
from jax.sharding import PartitionSpec as P

SEGLEN = 8192


def shifted(value, axis, steps):
    count = lax.axis_size(axis)
    first, last = (max(0, -steps), min(count, count - steps))
    return lax.ppermute(value, axis, [(source, source + steps) for source in range(first, last)])


def make_table(bin_ids):
    step = 2.0 * math.pi / SEGLEN
    low = lax.iota(jnp.int32, 128)
    high = lax.iota(jnp.int32, SEGLEN // 128) * 128
    low_angle = step * (bin_ids[:, None] * low[None, :] % SEGLEN).astype(jnp.float32)
    high_angle = step * (bin_ids[:, None] * high[None, :] % SEGLEN).astype(jnp.float32)
    cl, sl = jnp.cos(low_angle)[:, None, :], jnp.sin(low_angle)[:, None, :]
    ch, sh = jnp.cos(high_angle)[:, :, None], jnp.sin(high_angle)[:, :, None]
    window = 0.5 - 0.5 * jnp.cos(step * lax.iota(jnp.int32, SEGLEN).astype(jnp.float32))
    win = window.reshape(1, -1, 128)
    real = win * (ch * cl - sh * sl)
    imag = -win * (sh * cl + ch * sl)
    table = jnp.concatenate([real, imag], axis=0).astype(jnp.bfloat16)
    return (table.reshape(-1, 2, SEGLEN // 2), jnp.sum(window * window))


def per_device(records, bins, loads):
    highest = lax.Precision.HIGHEST
    tm_count = lax.axis_size("tm")
    all_bins = lax.all_gather(bins, "freq", axis=0, tiled=True)
    whole = lax.all_gather(loads, "tm", axis=2, tiled=True)
    table, energy = make_table(all_bins)
    half = SEGLEN // 2
    chans = records.shape[1]
    segs = records.shape[0] // half
    nbins = all_bins.shape[0]
    halves = records.reshape(segs, half, chans)
    both = jnp.concatenate([table[:, 0], table[:, 1]], axis=0)
    terms = jnp.einsum("kn,snc->skc", both, halves, preferred_element_type=jnp.float32)
    front, back = terms[:, : 2 * nbins], terms[:, 2 * nbins :]
    following = shifted(back[0], "tm", -1)
    spec = front + jnp.concatenate([back[1:], following[None]], axis=0)
    spectra = spec.reshape(segs, 2, nbins, chans).astype(jnp.bfloat16)
    owned = lax.all_to_all(spectra, "freq", split_axis=2, concat_axis=3, tiled=True)
    everything = lax.all_gather(owned, "tm", axis=0, tiled=True)
    rows = loads.shape[2]
    mine = lax.dynamic_slice_in_dim(everything, lax.axis_index("tm") * rows, rows, 3)
    scale = 1.0 / (segs * tm_count * energy)
    turned = jnp.stack([mine[:, 1], -mine[:, 0]], axis=1)
    left = jnp.stack([mine, turned], axis=0)
    csd = jnp.einsum("rspbi,spbj->ibrj", left, everything, preferred_element_type=jnp.float32) * scale
    hx_ra = jnp.einsum("hmj,spbj->hspbm", whole, everything, preferred_element_type=jnp.float32)
    y_real = hx_ra[0, :, 0] - hx_ra[1, :, 1]
    y_imag = hx_ra[0, :, 1] + hx_ra[1, :, 0]
    y = jnp.stack([y_real, y_imag], axis=1)
    count = y.shape[3] // tm_count
    ym = lax.dynamic_slice_in_dim(y, lax.axis_index("tm") * count, count, 3)
    yt = jnp.stack([ym, jnp.stack([ym[:, 1], -ym[:, 0]], axis=1)], axis=0)
    psd = jnp.einsum("rspbl,spbm->rblm", yt, y, precision=highest) * scale
    return (csd, psd)


def solution(mesh):
    placed = (P("tm", "freq"), P("freq"), P(None, None, "tm"))
    return jax.shard_map(
        per_device,
        mesh=mesh,
        in_specs=placed,
        out_specs=(P("tm", "freq", None, None), P(None, "freq", "tm", None)),
        check_vma=False,
    )
```

time: 629 us -> 127 us (0.20)
  waiting for transfers between devices: 407 us -> 25.4 us
  matrix products: 88.4 us -> 22.2 us
  other arithmetic: 49.8 us -> 3.9 us
  local copies, waits for them, and re-layouts: 42.5 us -> 19.4 us
  blocking collectives: 20.2 us -> 38.8 us
    reduce_scatter x2 -> x0, waiting for transfers between devices: 394 us -> none  [the longest x1 373 us: per_device(): lax.psum_scatter(cross_rows(owned, owned) * scale, 'tm', scatter_dimensio...]
    dot_general x11 -> x4, matrix products: 88.4 us -> 22.2 us  [the longest x1 13 us: per_device(): jnp.einsum('kn,snc->skc', both, halves, preferred_element_type=jnp.float32)]
    mul x1, other arithmetic: 44.5 us -> 0.01 us  [make_table(): high = lax.iota(jnp.int32, SEGLEN // 128) * 128]
    all_gather x0 -> x1, waiting for transfers between devices: none -> 23.6 us  [per_device(): everything = lax.all_gather(owned, 'tm', axis=0, tiled=True)]
    slice x2 -> x1, local copies, waits for them, and re-layouts: 23.1 us -> 0.07 us  [per_device(): spec = front + jnp.concatenate([back[1:], following[None]], axis=0)]
    all_to_all x0 -> x1, blocking collectives: none -> 17.5 us  [per_device(): lax.all_to_all(spectra, 'freq', split_axis=2, concat_axis=3, tiled=True)]
    all_to_all x1 -> x0, waiting for transfers between devices: 12.5 us -> none  [per_device(): lax.all_to_all(spectra, 'freq', split_axis=2, concat_axis=3, tiled=True)]
    unnamed x11 -> x10, local copies, waits for them, and re-layouts: 16.2 us -> 16 us
  transfers between devices with their start and end apart: 4 -> 2, of which waited for: 3 -> 2; matrix products, arithmetic and copies ran while one was open for 6% -> 1% of each run, Pallas kernels for 0% -> 0%
where the time goes in v1:
time: 127 us
  blocking collectives  38.8 us (31%)
  waiting for transfers between devices  25.4 us (20%)
  matrix products  22.2 us (17%)
  local copies, waits for them, and re-layouts  19.4 us (15%)
  between operations  15.6 us (12%)
  other arithmetic  3.9 us (3%)
  starting transfers between devices  1.33 us (1%)
    all_gather x1, waiting for transfers between devices, per_device(): everything = lax.all_gather(owned, 'tm', axis=0, tiled=True)  23.6 us
    all_to_all x1, blocking collectives, per_device(): lax.all_to_all(spectra, 'freq', split_axis=2, concat_axis=3, tiled=True)  17.5 us
    unnamed x10, local copies, waits for them, and re-layouts  16 us
    dot_general x1, matrix products, per_device(): jnp.einsum('kn,snc->skc', both, halves, preferred_element_type=jnp.float32)  13 us
    all_gather x1, blocking collectives, per_device(): whole = lax.all_gather(loads, 'tm', axis=2, tiled=True)  11.3 us
    unnamed x1, blocking collectives  9.89 us
    dot_general x1, matrix products, per_device(): jnp.einsum('rspbi,spbj->ibrj', left, everything, preferred_element_type=j...  4.83 us
    dot_general x1, matrix products, per_device(): jnp.einsum('hmj,spbj->hspbm', whole, everything, preferred_element_type=j...  3.84 us
  transfers between devices with their start and end apart: 2, of which 2 were waited for; matrix products, arithmetic and copies ran while one was open for 1% of the time, Pallas kernels for 0%

profile of v1, /device:TPU:0, one launch (start us, length us, event | category | flops | bytes accessed | tf_op | source)
XLA Modules:
  0.0 126.6 jit_solution(14870923464796908257)
XLA Ops:
  7.3 1.2 dynamic-slice
  9.2 0.9 dynamic-update-slice
  10.0 9.9 %all-reduce = s32[32]{0:T(128)S(1)} all-reduce(s32[32]{0:T(128)S(1)} %dynamic-update-slice), channel_id=1, replica_groups=mesh['tm'=8,'freq'=4] {'freq'}, use_global_device_ids=true, to_apply=%add | all-reduce | flops 32 | bytes 256
  20.3 0.6 multiply_subtract_fusion
  20.9 0.6 sub.39
  21.5 0.6 add.69
  22.1 0.5 fusion.51
  22.5 1.2 fusion.18
  23.8 13.0 %convolution_bitcast_fusion = f32[16,128,256]{2,1,0:T(8,128)S(1)} fusion(bf16[16,4096,256]{2,1,0:T(8,128)(2,1)} %bitcast.100, bf16[64,4096]{1,0:T(8,128)(2,1)S(1)} %get-tuple-element.13, bf16[64,4096]{1,0:T(8,128)(2,1)S(1)} %get-tuple-element.12), kind=kOutput, calls=%fused_computation.6 | convolution fusion | flops 4297064448 | bytes 36700160 | tf_op jit(solution)/shard_map/kn,snc->skc/dot_general | solution.py:45
  36.8 1.3 %collective-permute-start = (f32[64,256]{1,0:T(8,128)S(1)}, f32[64,256]{1,0:T(8,128)S(1)}, u32[]{:S(2)}, u32[]{:S(2)}) collective-permute-start(f32[64,256]{1,0:T(8,128)S(1)} %slice_bitcast_fusion.2), channel_id=1, source_target_pairs={{4,0},{8,4},{12,8},{16,12},{20,16},{24,20},{28,24},{5,1},{9,5},{13... | collective-permute-start | bytes 196616 | tf_op jit(solution)/shard_map/ppermute | solution.py:14
  38.2 1.8 %collective-permute-done = f32[64,256]{1,0:T(8,128)S(1)} collective-permute-done((f32[64,256]{1,0:T(8,128)S(1)}, f32[64,256]{1,0:T(8,128)S(1)}, u32[]{:S(2)}, u32[]{:S(2)}) %collective-permute-start) | collective-permute-done | bytes 65568 | tf_op jit(solution)/shard_map/ppermute | solution.py:14
  39.9 0.2 fusion.12
  40.1 0.5 copy.25
  40.7 17.5 %all_to_all.18 = bf16[16,2,32,256]{3,1,0,2:T(2,128)(2,1)S(1)} all-to-all(bf16[16,2,32,256]{3,1,0,2:T(2,128)(2,1)S(1)} %copy.25), channel_id=1, replica_groups=mesh['tm'=8,'freq'=4] {'freq'}, dimensions={2} | all-to-all | bytes 1048576 | tf_op jit(solution)/shard_map/all_to_all | solution.py:50
  58.2 0.4 copy.64
  58.7 1.2 all_to_all.16
  59.8 0.7 multiply_reduce_fusion
  61.3 11.3 %all_gather.11 = bf16[2,64,1024]{2,1,0:T(8,128)(2,1)S(1)} all-gather(bf16[2,64,128]{2,1,0:T(8,128)(2,1)S(1)} %copy-done.1), channel_id=1, replica_groups=mesh['tm'=8,'freq'=4] {'tm'}, dimensions={2}, use_global_device_ids=true | all-gather | bytes 294912 | tf_op jit(solution)/shard_map/all_gather | solution.py:37
  72.6 23.6 %all-gather.2.cloned.1.call-done = bf16[128,2,8,1024]{3,0,1,2:T(8,128)(2,1)} async-done(((bf16[16,2,8,1024]{3,0,1,2:T(8,128)(2,1)}), bf16[128,2,8,1024]{3,0,1,2:T(8,128)(2,1)}) %all-gather.2.cloned.1.call-update) | async-done | bytes 4194320 | tf_op jit(solution)/shard_map/all_gather | solution.py:51
  96.2 3.8 %fusion.7 = f32[2,128,2,8,64]{1,4,0,3,2:T(8,128)S(1)} fusion(bf16[2,64,1024]{2,1,0:T(8,128)(2,1)S(1)} %all_gather.11, bf16[128,2,8,1024]{3,0,1,2:T(8,128)(2,1)} %all-gather.2.cloned.1.call-done), kind=kOutput, calls=%fused_computation.7 | convolution fusion | flops 536870912 | bytes 5505024 | tf_op jit(solution)/shard_map/hmj,spbj->hspbm/dot_general | solution.py:58
  100.2 0.6 fusion.11
  100.8 0.6 copy.33
  101.8 4.8 %fusion = f32[128,8,2,1024]{0,3,2,1:T(8,128)} fusion(f32[]{:T(128)S(6)} %div.3, bf16[128,2,8,1024]{3,0,1,2:T(8,128)(2,1)S(1)} %copy-done, bf16[1,128,2,8,128]{4,1,2,0,3:T(8,128)(2,1)S(1)} %maximum_bitcast_fusion.2, bf16[1,128,2,8,128]{4,1,2,0,3:T(8,128)(2,1)S(1)} %dynamic-slice_bitcast_fusion), kind=kOutput, calls=%fused_computation.1 | convolution fusion | flops 1077936128 | bytes 13631492 | tf_op jit(solution)/shard_map/rspbi,spbj->ibrj/dot_general | solution.py:57
  106.6 13.2 %copy.32 = f32[128,8,2,1024]{3,2,1,0:T(2,128)} copy(f32[128,8,2,1024]{0,3,2,1:T(8,128)} %fusion) | data formatting | bytes 16777216
  (25 shorter events, 1.1 us)
Async XLA Ops:
  7.2 89.0 %all-gather.2.cloned.1.call-start = ((), (), s32[]{:S(2)}) async-start(), calls=%async_computation.1 | async-start | bytes 4718592 | tf_op jit(solution)/shard_map/all_gather | solution.py:51
  36.8 24.5 %copy-start.1 = (bf16[2,64,128]{2,1,0:T(8,128)(2,1)S(1)}, bf16[2,64,128]{2,1,0:T(8,128)(2,1)}, u32[]{:S(2)}) copy-start(bf16[2,64,128]{2,1,0:T(8,128)(2,1)} %param.5) | copy-start | bytes 98308
  36.8 3.1 %collective-permute-start = (f32[64,256]{1,0:T(8,128)S(1)}, f32[64,256]{1,0:T(8,128)S(1)}, u32[]{:S(2)}, u32[]{:S(2)}) collective-permute-start(f32[64,256]{1,0:T(8,128)S(1)} %slice_bitcast_fusion.2), channel_id=1, source_target_pairs={{4,0},{8,4},{12,8},{16,12},{20,16},{24,20},{28,24},{5,1},{9,5},{13... | collective-permute-start | bytes 196616 | tf_op jit(solution)/shard_map/ppermute | solution.py:14
  96.2 5.2 %copy-start = (bf16[128,2,8,1024]{3,0,1,2:T(8,128)(2,1)S(1)}, bf16[128,2,8,1024]{3,0,1,2:T(8,128)(2,1)}, u32[]{:S(2)}) copy-start(bf16[128,2,8,1024]{3,0,1,2:T(8,128)(2,1)} %all-gather.2.cloned.1.call-done) | copy-start | bytes 12582916
Sparse Core Ops, SparseCore 0:
  60.0 36.1 all-gather.1

commit v2 on v1

v2 whole, which is shorter than its diff:
```python
import functools
import math

import jax
import jax.numpy as jnp
import numpy as np
from jax import lax
from jax.experimental import pallas as pl
from jax.experimental.pallas import tpu as pltpu
from jax.sharding import PartitionSpec as P

SEGLEN = 8192
HALF = SEGLEN // 2
MESH = pl.DeviceIdType.MESH
MIB = 1 << 20


def window_of():
    return 0.5 - 0.5 * np.cos(2.0 * np.pi / SEGLEN * np.arange(SEGLEN))


def flipped(index, bits):
    for bit in bits:
        index = index + bit * (1 - 2 * ((index // bit) % 2))
    return index


def bits_of(number):
    return [1 << at for at in range(number.bit_length()) if number >> at & 1]


def spectra_kernel(
    shape, records_ref, bins_ref, loads_ref, window_ref, out_ref, all_loads_ref,
    rec, all_bins, table, front, halo_out, halo, spec, gathered, loads_buf,
    rec_sem, bin_send, bin_recv, load_send, load_recv, halo_sems, local_sem,
    z_send, z_recv, t_send, t_recv, out_sem, loads_sem,
):
    times, freqs, segs, own, chans, chunks = shape
    t, f = lax.axis_index("tm"), lax.axis_index("freq")
    rows = freqs * 2 * own
    size = segs // chunks

    def fetch(j):
        start = j * HALF if isinstance(j, int) else pl.multiple_of(j * HALF, HALF)
        return pltpu.make_async_copy(records_ref.at[pl.ds(start, HALF)], rec.at[j], rec_sem.at[j])

    for j in range(segs):
        fetch(j).start()

    row = lax.broadcasted_iota(jnp.int32, (own, 128), 0)
    held_bins = jnp.zeros((own, 128), jnp.int32)
    for q in range(own):
        held_bins = jnp.where(row == q, bins_ref[q], held_bins)
    all_bins[f] = held_bins
    held_rows = loads_ref.shape[1]
    if held_rows % 128:
        loads_slot = loads_buf.at[t]
    else:
        loads_slot = loads_buf.at[:, pl.ds(pl.multiple_of(t * held_rows, held_rows), held_rows)]

    barrier = pltpu.get_barrier_semaphore()
    for d in range(1, times):
        pl.semaphore_signal(barrier, inc=1, device_id={"tm": lax.rem(t + d, times)}, device_id_type=MESH)
    for e in range(1, freqs):
        pl.semaphore_signal(barrier, inc=1, device_id={"freq": lax.rem(f + e, freqs)}, device_id_type=MESH)
    pl.semaphore_wait(barrier, times + freqs - 2)

    sends = []
    bin_copies = []
    for e in range(1, freqs):
        copy = pltpu.make_async_remote_copy(
            all_bins.at[f], all_bins.at[f], bin_send.at[e], bin_recv.at[e],
            device_id={"freq": lax.rem(f + e, freqs)}, device_id_type=MESH)
        copy.start()
        bin_copies.append(copy)
    load_copies = []
    for d in range(1, times):
        copy = pltpu.make_async_remote_copy(
            loads_ref, loads_slot, load_send.at[d], load_recv.at[d],
            device_id={"tm": lax.rem(t + d, times)}, device_id_type=MESH)
        copy.start()
        load_copies.append(copy)
    loads_slot[...] = loads_ref[...]

    @pl.when(t == times - 1)
    def _():
        halo[...] = jnp.zeros_like(halo)

    for copy in bin_copies:
        copy.wait()

    step = 2.0 * math.pi / SEGLEN
    ks = all_bins[...].reshape(freqs * own, 128)
    lane = lax.broadcasted_iota(jnp.int32, ks.shape, 1)
    low = step * ((ks * lane) & (SEGLEN - 1)).astype(jnp.float32)
    high = step * ((ks * lane * 128) & (SEGLEN - 1)).astype(jnp.float32)
    cl, sl, ch, sh = jnp.cos(low), jnp.sin(low), jnp.cos(high), jnp.sin(high)
    blocks = HALF // 128
    for h in range(2 * blocks):
        w = window_ref[h : h + 1, :]
        c1, s1 = ch[:, h : h + 1], sh[:, h : h + 1]
        real = w * (c1 * cl - s1 * sl)
        imag = -w * (s1 * cl + c1 * sl)
        parts = jnp.concatenate(
            [real.reshape(freqs, 1, own, 128), imag.reshape(freqs, 1, own, 128)], axis=1
        ).reshape(rows, 128)
        at = h // blocks * rows
        table[at : at + rows, h % blocks * 128 : (h % blocks + 1) * 128] = parts.astype(jnp.bfloat16)

    def transform(j):
        fetch(j).wait()
        return jnp.dot(table[...], rec[j], preferred_element_type=jnp.float32)

    def keep(j, value):
        value = value.astype(jnp.bfloat16)
        for g in range(freqs):
            spec[g, j] = value[g * 2 * own : (g + 1) * 2 * own]

    first = transform(0)
    front[...] = first[:rows]
    halo_out[...] = first[rows:]

    def halo_copy():
        return pltpu.make_async_remote_copy(
            halo_out, halo, halo_sems.at[0], halo_sems.at[1],
            device_id={"tm": jnp.maximum(t - 1, 0)}, device_id_type=MESH)

    @pl.when(t > 0)
    def _():
        halo_copy().start()

    def body(j, carry):
        terms = transform(j)
        keep(j - 1, front[...] + terms[rows:])
        front[...] = terms[:rows]
        return carry

    columns = pl.ds(pl.multiple_of(f * chans, chans), chans)
    highs = [1 << at for at in range(1, (times - 1).bit_length())]
    orders = []
    for c in range(chunks):
        turn = c % max(len(highs), 1)
        orders.append(highs[turn:] + highs[:turn] + [1])
    stages = len(orders[0])

    def span(c):
        return pl.ds(c * size, size)

    z_copies, t_copies, locals_ = {}, {}, {}

    def send_t(c, held, bit):
        block = gathered.at[flipped(t, bits_of(held)), span(c)]
        copy = pltpu.make_async_remote_copy(
            block, block, t_send.at[c, held | bit], t_recv.at[c, held | bit],
            device_id={"tm": flipped(t, [bit])}, device_id_type=MESH)
        copy.start()
        t_copies[c, held | bit] = copy

    def top(order, held):
        return max(at for at, bit in enumerate(order) if held & bit)

    for at in range(chunks + stages + 1):
        if at < chunks:
            c = at
            lax.fori_loop(c * size + 1, min((c + 1) * size, segs - 1) + 1, body, 0)
            if c == chunks - 1:
                @pl.when(t < times - 1)
                def _():
                    halo_copy().wait_recv()
                keep(segs - 1, front[...] + halo[...])
            for e in range(1, freqs):
                peer = lax.rem(f + e, freqs)
                copy = pltpu.make_async_remote_copy(
                    spec.at[peer, span(c)], gathered.at[t, span(c), :, columns],
                    z_send.at[c, e], z_recv.at[c, e],
                    device_id={"freq": peer}, device_id_type=MESH)
                copy.start()
                z_copies[c, e] = copy
            locals_[c] = pltpu.make_async_copy(
                spec.at[f, span(c)], gathered.at[t, span(c), :, columns], local_sem.at[c])
            locals_[c].start()
        for c in range(chunks):
            stage = at - 1 - c
            if stage < 0 or stage > stages:
                continue
            order = orders[c]
            if stage == 0:
                locals_[c].wait()
                for e in range(1, freqs):
                    z_copies[c, e].wait_recv()
                for bit in order:
                    send_t(c, 0, bit)
                continue
            for held in range(1, times):
                if top(order, held) == stage - 1:
                    t_copies[c, held].wait_recv()
                    for bit in order[stage:]:
                        send_t(c, held, bit)
            if stage == stages:
                pltpu.make_async_copy(gathered.at[:, span(c)], out_ref.at[:, span(c)], out_sem.at[c]).start()

    for copy in load_copies:
        copy.wait()
    loads_out = pltpu.make_async_copy(loads_buf, all_loads_ref, loads_sem)
    loads_out.start()

    @pl.when(t > 0)
    def _():
        halo_copy().wait_send()

    for copy in list(z_copies.values()) + list(t_copies.values()):
        copy.wait_send()
    for c in range(chunks):
        pltpu.make_async_copy(gathered.at[:, span(c)], out_ref.at[:, span(c)], out_sem.at[c]).wait()
    loads_out.wait()


def gather_spectra(records, bins, loads):
    times, freqs = lax.axis_size("tm"), lax.axis_size("freq")
    segs, own, chans = records.shape[0] // HALF, bins.shape[0], records.shape[1]
    chunks = 4
    rows = freqs * 2 * own
    count, held = 2 * loads.shape[1], loads.shape[2]
    gathered_loads = (times, count, held) if held % 128 else (count, times * held)
    window = jnp.asarray(window_of().reshape(-1, 128), jnp.float32)
    dma = pltpu.SemaphoreType.DMA
    smem = pl.BlockSpec(memory_space=pltpu.SMEM)
    anywhere, vmem = pl.BlockSpec(memory_space=pl.ANY), pl.BlockSpec(memory_space=pltpu.VMEM)
    return pl.pallas_call(
        functools.partial(spectra_kernel, (times, freqs, segs, own, chans, chunks)),
        out_shape=(
            jax.ShapeDtypeStruct((times, segs, 2 * own, freqs * chans), jnp.bfloat16),
            jax.ShapeDtypeStruct(gathered_loads, jnp.bfloat16),
        ),
        in_specs=[anywhere, smem, vmem, vmem],
        out_specs=(anywhere, anywhere),
        scratch_shapes=[
            pltpu.VMEM((segs, HALF, chans), jnp.bfloat16),
            pltpu.VMEM((freqs, own, 128), jnp.int32),
            pltpu.VMEM((2 * rows, HALF), jnp.bfloat16),
            pltpu.VMEM((rows, chans), jnp.float32),
            pltpu.VMEM((rows, chans), jnp.float32),
            pltpu.VMEM((rows, chans), jnp.float32),
            pltpu.VMEM((freqs, segs, 2 * own, chans), jnp.bfloat16),
            pltpu.VMEM((times, segs, 2 * own, freqs * chans), jnp.bfloat16),
            pltpu.VMEM(gathered_loads, jnp.bfloat16),
            dma((segs,)), dma((freqs,)), dma((freqs,)), dma((times,)), dma((times,)), dma((2,)), dma((chunks,)),
            dma((chunks, freqs)), dma((chunks, freqs)), dma((chunks, times)), dma((chunks, times)),
            dma((chunks,)), dma(()),
        ],
        compiler_params=pltpu.CompilerParams(
            collective_id=0, has_side_effects=True, vmem_limit_bytes=56 * MIB),
        name="spectra",
    )(records, bins, loads.reshape(count, -1), window)


def csd_kernel(scale, own, all_ref, loads_ref, mine_ref, csd_ref, psd_ref, wide, wide_mine, applied, held):
    b = pl.program_id(0)
    tiles, depth = wide.shape[0], wide.shape[1] // (2 * own)
    rows, count = csd_ref.shape[0], loads_ref.shape[0] // 2
    over_rows = (((0,), (0,)), ((), ()))

    @pl.when(b == 0)
    def _():
        for c in range(tiles):
            wide[c] = all_ref[:, c * 128 : (c + 1) * 128].astype(jnp.float32)
        if wide_mine is not None:
            wide_mine[...] = mine_ref[...].astype(jnp.float32)
        applied[...] = lax.dot_general(
            all_ref[...], loads_ref[...], (((1,), (1,)), ((), ())), preferred_element_type=jnp.float32)

    real_at, imag_at = pl.ds(b, depth, stride=2 * own), pl.ds(own + b, depth, stride=2 * own)
    t = lax.axis_index("tm")
    if wide_mine is None:
        mine_a, mine_b = wide[t, real_at, :], wide[t, imag_at, :]
    else:
        mine_a, mine_b = wide_mine[real_at, :], wide_mine[imag_at, :]
    left = (jnp.concatenate([mine_a, mine_b], axis=0).astype(jnp.bfloat16),
            jnp.concatenate([mine_b, -mine_a], axis=0).astype(jnp.bfloat16))
    flat = csd_ref.reshape(rows * 2 * tiles, 128)
    for c in range(0, tiles, 2):
        right = jnp.concatenate([
            jnp.concatenate([wide[c, real_at, :], wide[c, imag_at, :]], axis=0),
            jnp.concatenate([wide[c + 1, real_at, :], wide[c + 1, imag_at, :]], axis=0),
        ], axis=1).astype(jnp.bfloat16)
        for p in range(2):
            value = lax.dot_general(left[p], right, over_rows, preferred_element_type=jnp.float32) * scale
            for u in range(2):
                flat[pl.ds(2 * (c + u) + p, rows, stride=2 * tiles), :] = value[:rows, u * 128 : (u + 1) * 128]

    ya, yb = applied[real_at, :], applied[imag_at, :]
    y_real = ya[:, :count] - yb[:, count:]
    y_imag = yb[:, :count] + ya[:, count:]
    y = jnp.concatenate([y_real, y_imag], axis=0)
    turned = jnp.concatenate([y_imag, -y_real], axis=0)
    for p, part in enumerate((y, turned)):
        held[...] = scale * lax.dot_general(
            part, y, over_rows, precision=lax.Precision.HIGHEST, preferred_element_type=jnp.float32)
        share = psd_ref.shape[1]
        psd_ref[p] = held[pl.ds(t * share, share), :]


def csd_aligned(scale, own, all_ref, loads_ref, csd_ref, psd_ref, wide, applied, held):
    csd_kernel(scale, own, all_ref, loads_ref, None, csd_ref, psd_ref, wide, None, applied, held)


def per_device(records, bins, loads):
    times = lax.axis_size("tm")
    t = lax.axis_index("tm")
    own, (_, count, rows) = bins.shape[0], loads.shape
    gathered, all_loads = gather_spectra(records, bins, loads)
    _, segs, _, cols = gathered.shape
    everything = gathered.reshape(-1, cols)
    aligned = rows == 128
    if rows % 128:
        whole = all_loads.transpose(1, 0, 2).reshape(2 * count, cols)
    else:
        whole = all_loads
    operands = [everything, whole]
    if not aligned:
        mine = lax.dynamic_slice_in_dim(everything, t * rows, rows, 1)
        operands.append(jnp.pad(mine, ((0, 0), (0, -rows % 128))))
    scale = float(1.0 / (segs * times * np.sum(window_of() ** 2)))
    tiles = cols // 128
    total, share = everything.shape[0], count // times
    full = lambda shape: pl.BlockSpec(shape, lambda b: (0, 0))
    csd, psd = pl.pallas_call(
        functools.partial(csd_aligned if aligned else csd_kernel, scale, own),
        grid=(own,),
        out_shape=(
            jax.ShapeDtypeStruct((rows, own, 2 * tiles, 128), jnp.float32),
            jax.ShapeDtypeStruct((2, own, share, count), jnp.float32),
        ),
        in_specs=[full(operand.shape) for operand in operands],
        out_specs=(
            pl.BlockSpec((rows, None, 2 * tiles, 128), lambda b: (0, b, 0, 0)),
            pl.BlockSpec((2, None, share, count), lambda b: (0, b, 0, 0)),
        ),
        scratch_shapes=[
            pltpu.VMEM((tiles, total, 128), jnp.float32),
            *([] if aligned else [pltpu.VMEM(operands[2].shape, jnp.float32)]),
            pltpu.VMEM((total, 2 * count), jnp.float32),
            pltpu.VMEM((count, count), jnp.float32),
        ],
        compiler_params=pltpu.CompilerParams(vmem_limit_bytes=56 * MIB),
        name="csd",
    )(*operands)
    csd = csd.reshape(rows, own, tiles, 2, 128).transpose(0, 1, 3, 2, 4).reshape(rows, own, 2, cols)
    return (csd, psd)


def solution(mesh):
    placed = (P("tm", "freq"), P("freq"), P(None, None, "tm"))
    return jax.shard_map(
        per_device,
        mesh=mesh,
        in_specs=placed,
        out_specs=(P("tm", "freq", None, None), P(None, "freq", "tm", None)),
        check_vma=False,
    )
```

time: 127 us -> 63.1 us (0.50)
  Pallas kernels: 0 us -> 61.4 us
  blocking collectives: 38.8 us -> 0 us
  waiting for transfers between devices: 25.4 us -> 0 us
  matrix products: 22.2 us -> 0 us
  local copies, waits for them, and re-layouts: 19.4 us -> 0 us
  between operations: 15.6 us -> 0.64 us
  other arithmetic: 3.9 us -> 0 us
  starting transfers between devices: 1.33 us -> 0 us
    pallas_call x0 -> x2, Pallas kernels: none -> 61.4 us  [the longest x1 46.9 us: gather_spectra(): pl.pallas_call(functools.partial(spectra_kernel, (times, freqs, segs, own...]
    all_gather x1 -> x0, waiting for transfers between devices: 23.6 us -> none  [per_device(): everything = lax.all_gather(owned, 'tm', axis=0, tiled=True)]
    dot_general x4 -> x0, matrix products: 22.2 us -> none  [the longest x1 13 us: per_device(): jnp.einsum('kn,snc->skc', both, halves, preferred_element_type=jnp.float32)]
    all_to_all x1 -> x0, blocking collectives: 17.5 us -> none  [per_device(): lax.all_to_all(spectra, 'freq', split_axis=2, concat_axis=3, tiled=True)]
    unnamed x10 -> x0, local copies, waits for them, and re-layouts: 16 us -> none
    all_gather x1 -> x0, blocking collectives: 11.3 us -> none  [per_device(): whole = lax.all_gather(loads, 'tm', axis=2, tiled=True)]
    unnamed x1 -> x0, blocking collectives: 9.89 us -> none
    ppermute x1 -> x0, waiting for transfers between devices: 1.78 us -> none  [shifted(): lax.ppermute(value, axis, [(source, source + steps) for source in range(f...]
  transfers between devices with their start and end apart: 2 -> 0, of which waited for: 2 -> 0; matrix products, arithmetic and copies ran while one was open for 1% -> 0% of each run, Pallas kernels for 0% -> 0%
where the time goes in v2:
time: 63.1 us; the launch traced here: 62 us
  Pallas kernels  61.4 us (97%)
  between operations  0.64 us (1%)
    pallas_call x1, Pallas kernels, gather_spectra(): pl.pallas_call(functools.partial(spectra_kernel, (times, freqs, segs, own...  46.9 us
    pallas_call x1, Pallas kernels, per_device(): pl.pallas_call(functools.partial(csd_aligned if aligned else csd_kernel,...  14.5 us

profile of v2, /device:TPU:0, one launch (start us, length us, event | category | flops | bytes accessed | tf_op | source)
XLA Modules:
  0.0 62.0 jit_solution(13316653620111679205)
XLA Ops:
  0.6 46.9 %spectra.1 = (bf16[8,16,16,1024]{3,2,1,0:T(8,128)(2,1)}, bf16[128,1024]{1,0:T(8,128)(2,1)}) custom-call(bf16[65536,256]{1,0:T(8,128)(2,1)} %records_ref.1, s32[8]{0:T(128)} %bins_ref.1, bf16[128,128]{1,0:T(8,128)(2,1)} %bitcast.8, f32[64,128]{1,0:T(8,128)} %constant.2.clone.window_ref), custom_call_target="tpu_custom_call" | custom-call | tf_op jit(solution)/shard_map/spectra/pallas_call | solution.py:229
  47.5 14.5 %csd.1 = (f32[128,8,16,128]{3,2,1,0:T(8,128)}, f32[2,8,8,64]{3,2,1,0:T(8,128)}) custom-call(bf16[2048,1024]{1,0:T(8,128)(2,1)} %bitcast.7, bf16[128,1024]{1,0:T(8,128)(2,1)} %get-tuple-element.7.loads_ref), custom_call_target="tpu_custom_call" | custom-call | tf_op jit(solution)/shard_map/csd/pallas_call | solution.py:327
